TPU v7x, 32 devices: a whole 2x2x4 slice. The times are simulated.
32 devices in a mesh: groups: 2 (over x), wide: 16 (over z, y, core).
Axes of the slice: x: 2, y: 2, z: 4, core: 2. Of those that a mesh axis runs over, the one named last changes fastest.
Arguments:
- hidden_in: bfloat16 [32, 16384], P(('groups', 'wide')), parts along dimension 0, may hold values from -6 to 6
- norm_gain: float32 [16384], replicated, may hold values from 0.5 to 2
- query_weight: bfloat16 [16384, 16384], P(None, 'wide'), may hold values from -0.046875 to 0.046875
- kv_weight: bfloat16 [16384, 2048], P(None, 'wide'), may hold values from -0.046875 to 0.046875
- out_weight: bfloat16 [16384, 16384], P('wide'), may hold values from -0.75 to 0.75
- cache_keys: bfloat16 [32, 512, 1024], P(('groups', 'wide')), parts along dimension 0, may hold values from -64 to 64
- cache_values: bfloat16 [32, 512, 1024], P(('groups', 'wide')), parts along dimension 0, may hold values from -6 to 6
- lengths: int32 [32], P(('groups', 'wide')), parts along dimension 0, may hold values from 1 to 512, 5120 in all
- positions: int32 [32], P(('groups', 'wide')), parts along dimension 0, may hold values from 512 to 8191
Outputs:
- hidden_out: bfloat16 [32, 16384], P(('groups', 'wide')), parts along dimension 0
There are 2 independent parts, one for each index of `groups`. A program takes and returns all parts, laid end to end along the dimension named above; an argument that names none is the same for every part. Nothing has to cross between parts.
Inputs may be any that keep to these rules, and one draw needn't show every extreme that they name: `lengths`: some request has all 512 slots filled.
All inputs are finite; a program needn't handle non-finite values. No bound on the sum of `lengths` on one device may be relied on, other than what follows from the above.
Results may differ from a plain program's by a relative error of at most 0.012.
The roundings to bfloat16 on the way count: a program that leaves them out, or rounds other values in their place, can miss the bound.
Values may be sent and summed in bfloat16 or wider, within the bound.
A program may use at most 192 MiB of HBM per device.

v0:
```python
import math

import jax
import jax.numpy as jnp
from jax import lax
from jax.sharding import PartitionSpec as P

HQ = 128
KVH = 8
HD = 128


def rms_scale(inputs_wide, norm_gain):
    spread = jnp.mean(inputs_wide * inputs_wide, axis=-1, keepdims=True)
    return inputs_wide * lax.rsqrt(spread + 1e-05) * norm_gain


def rotary(values, places, head_count, head_size):
    grouped = values.reshape(values.shape[0], head_count, head_size)
    halfway = head_size // 2
    indices = jnp.arange(halfway).astype(jnp.float32)
    inverse = jnp.exp(indices * (-2.0 * math.log(500000.0) / head_size))
    angles = places.astype(jnp.float32)[:, None] * inverse[None, :]
    cosine = jnp.cos(angles)[:, None, :]
    sine = jnp.sin(angles)[:, None, :]
    first = grouped[..., :halfway]
    second = grouped[..., halfway:]
    turned = jnp.concatenate(
        [first * cosine - second * sine, second * cosine + first * sine], axis=-1
    )
    return turned.reshape(values.shape)


def attend(query_rows, kv_rows, cache_keys, cache_values, lengths, positions):
    local_rows, slots = (cache_keys.shape[0], cache_keys.shape[1])
    group_size = HQ // KVH
    key_width = KVH * HD
    factor = 1.0 / math.sqrt(HD)
    queries = rotary(query_rows.astype(jnp.float32), positions, HQ, HD).astype(jnp.bfloat16)
    queries = queries.reshape(local_rows, KVH, group_size, HD)
    new_keys = rotary(kv_rows[:, :key_width].astype(jnp.float32), positions, KVH, HD).astype(
        jnp.bfloat16
    )
    new_keys = new_keys.reshape(local_rows, KVH, HD)
    new_values = kv_rows[:, key_width:].reshape(local_rows, KVH, HD)
    old_keys = cache_keys.reshape(local_rows, slots, KVH, HD)
    old_values = cache_values.reshape(local_rows, slots, KVH, HD)
    cached_scores = (
        jnp.einsum("rkgd,rlkd->rkgl", queries, old_keys, preferred_element_type=jnp.float32)
        * factor
    )
    fresh_scores = (
        jnp.einsum("rkgd,rkd->rkg", queries, new_keys, preferred_element_type=jnp.float32) * factor
    )
    visible = jnp.arange(slots)[None, :] < lengths[:, None]
    cached_scores = jnp.where(visible[:, None, None, :], cached_scores, -1e30)
    highest = jnp.maximum(jnp.max(cached_scores, axis=-1), fresh_scores)
    cached_exp = jnp.exp(cached_scores - highest[..., None])
    fresh_exp = jnp.exp(fresh_scores - highest)
    totals = jnp.sum(cached_exp, axis=-1) + fresh_exp
    cached_weights = (cached_exp / totals[..., None]).astype(jnp.bfloat16)
    fresh_weights = (fresh_exp / totals).astype(jnp.bfloat16)
    mixed_values = jnp.einsum(
        "rkgl,rlkd->rkgd", cached_weights, old_values, preferred_element_type=jnp.float32
    )
    mixed_values = (
        mixed_values
        + fresh_weights.astype(jnp.float32)[..., None]
        * new_values.astype(jnp.float32)[:, :, None, :]
    )
    return mixed_values.reshape(local_rows, HQ * HD).astype(jnp.bfloat16)


def per_device(
    hidden_in,
    norm_gain,
    query_weight,
    kv_weight,
    out_weight,
    cache_keys,
    cache_values,
    lengths,
    positions,
):
    inputs_wide = hidden_in.astype(jnp.float32)
    normed = rms_scale(inputs_wide, norm_gain).astype(jnp.bfloat16)
    query_cols = query_weight.shape[1]
    piece = lax.all_gather(normed, "wide", axis=0, tiled=True)
    query_part = jnp.dot(piece, query_weight, preferred_element_type=jnp.float32)
    fresh_part = jnp.dot(piece, kv_weight, preferred_element_type=jnp.float32)
    projected = jnp.concatenate([query_part, fresh_part], axis=1).astype(jnp.bfloat16)
    query_rows, kv_rows = (
        lax.all_to_all(projected[:, :query_cols], "wide", split_axis=0, concat_axis=1, tiled=True),
        lax.all_to_all(projected[:, query_cols:], "wide", split_axis=0, concat_axis=1, tiled=True),
    )
    attended = attend(query_rows, kv_rows, cache_keys, cache_values, lengths, positions)
    by_heads = lax.all_to_all(attended, "wide", split_axis=1, concat_axis=0, tiled=True)
    summed = lax.psum_scatter(
        jnp.dot(by_heads, out_weight, preferred_element_type=jnp.float32),
        "wide",
        scatter_dimension=0,
        tiled=True,
    )
    return (inputs_wide + summed).astype(jnp.bfloat16)


def solution(mesh):
    return jax.shard_map(
        per_device,
        mesh=mesh,
        in_specs=(
            P(("groups", "wide"), None),
            P(),
            P(None, "wide"),
            P(None, "wide"),
            P("wide", None),
            P(("groups", "wide"), None, None),
            P(("groups", "wide"), None, None),
            P(("groups", "wide")),
            P(("groups", "wide")),
        ),
        out_specs=P(("groups", "wide"), None),
        check_vma=False,
    )
```

profile of v0, /device:TPU:0, one launch (start us, length us, event | category | flops | bytes accessed | tf_op | source)
XLA Modules:
  0.0 197.7 jit_solution(15282218653755374183)
XLA Ops:
  6.5 1.7 multiply_reduce_fusion
  9.0 1.0 convert_bitcast_fusion
  9.9 26.2 %all-gather = bf16[16,1,16384]{2,1,0:T(2,128)(2,1)S(1)} all-gather(bf16[1,1,16384]{2,1,0:T(2,128)(2,1)S(1)} %convert_bitcast_fusion), channel_id=1, replica_groups=mesh['groups'=2,'wide'=16] {'wide'}, dimensions={0}, use_global_device_ids=true | all-gather | bytes 557056 | tf_op jit(solution)/shard_map/all_gather | solution.py:88
  36.2 3.1 %fusion.3 = bf16[16,1,128]{2,0,1:T(8,128)(2,1)S(1)} fusion(bf16[16384,128]{1,0:T(8,128)(2,1)} %param.12, bf16[16,1,16384]{2,1,0:T(2,128)(2,1)S(1)} %all-gather), kind=kOutput, calls=%fused_computation.7 | convolution fusion | flops 67110912 | bytes 4722688 | tf_op jit(solution)/shard_map/dot_general | solution.py:90
  39.3 0.6 copy.21
  39.9 3.5 %all-to-all-start.1 = ((bf16[16,1,128]{2,1,0:T(2,128)(2,1)}), bf16[16,1,128]{2,1,0:T(2,128)(2,1)S(1)}, u32[]{:S(2)}, u32[]{:S(2)}) async-start(bf16[16,1,128]{2,1,0:T(2,128)(2,1)} %copy.21), calls=%async_computation.1 | async-start | bytes 16384 | tf_op jit(solution)/shard_map/all_to_all | solution.py:94
  43.4 12.9 %fusion.2 = bf16[16,1,1024]{2,0,1:T(8,128)(2,1)S(1)} fusion(bf16[16384,1024]{1,0:T(8,128)(2,1)} %param.11, bf16[16,1,16384]{2,1,0:T(2,128)(2,1)S(1)} %all-gather), kind=kOutput, calls=%fused_computation.5 | convolution fusion | flops 536887296 | bytes 34111488 | tf_op jit(solution)/shard_map/dot_general | solution.py:89
  57.7 0.5 broadcast.58
  58.2 0.6 reduce.5
  58.7 0.6 reshape.201
  59.4 0.3 copy.28
  59.7 0.3 copy.29
  59.9 6.0 %all-to-all-start = ((bf16[16,2,512]{2,1,0:T(2,128)(2,1)}), bf16[16,2,512]{2,1,0:T(2,128)(2,1)S(1)}, u32[]{:S(2)}, u32[]{:S(2)}) async-start(bf16[16,2,512]{2,1,0:T(2,128)(2,1)} %reshape.201), calls=%async_computation | async-start | bytes 65536 | tf_op jit(solution)/shard_map/all_to_all | solution.py:93
  66.2 6.4 %all-to-all-done = bf16[16,2,512]{2,1,0:T(2,128)(2,1)S(1)} async-done(((bf16[16,2,512]{2,1,0:T(2,128)(2,1)}), bf16[16,2,512]{2,1,0:T(2,128)(2,1)S(1)}, u32[]{:S(2)}, u32[]{:S(2)}) %all-to-all-start) | async-done | bytes 32800 | tf_op jit(solution)/shard_map/all_to_all | solution.py:93
  72.9 0.1 fusion.17
  73.0 0.5 fusion.25
  73.5 0.2 fusion.8
  73.7 0.3 fusion.1
  74.1 0.7 reduce.6
  74.8 9.2 %all_to_all.42 = bf16[16,2,512]{2,1,0:T(2,128)(2,1)S(1)} all-to-all(bf16[16,2,512]{2,1,0:T(2,128)(2,1)S(1)} %reshape.203), channel_id=1, replica_groups=mesh['groups'=2,'wide'=16] {'wide'}, dimensions={0} | all-to-all | bytes 65536 | tf_op jit(solution)/shard_map/all_to_all | solution.py:97
  84.1 13.9 %fusion.14 = f32[16,16384]{1,0:T(8,128)} fusion(bf16[1024,16384]{1,0:T(8,128)(2,1)} %param.13, bf16[1,16,1024]{2,0,1:T(2,128)(2,1)S(1)} %bitcast.51), kind=kOutput, calls=%fused_computation.26 | convolution fusion | flops 536870912 | bytes 34635776 | tf_op jit(solution)/shard_map/dot_general | solution.py:99
  98.0 0.6 dynamic-slice
  98.6 89.9 %all-reduce.3.cloned.1.call-done = f32[16,16384]{1,0:T(8,128)} async-done(((f32[16,16384]{1,0:T(8,128)}), f32[16,16384]{1,0:T(8,128)}) %all-reduce.3.cloned.1.call-update) | async-done | bytes 1048592
  188.5 2.4 %fusion.13 = bf16[1,16384]{1,0:T(2,128)(2,1)} fusion(f32[16,16384]{1,0:T(8,128)} %all-reduce.3.cloned.1.call-done, u32[]{:T(128)} %bitcast.16, bf16[1,16384]{1,0:T(2,128)(2,1)S(1)} %copy-done.2), kind=kLoop, calls=%fused_computation.20 | loop fusion | flops 49152 | bytes 131076 | tf_op jit(solution)/shard_map/convert_element_type | solution.py:104
  (25 shorter events, 0.7 us)
Async XLA Ops:
  6.5 52.8 %copy-start = (bf16[1,512,1024]{2,1,0:T(8,128)(2,1)S(1)}, bf16[1,512,1024]{2,1,0:T(8,128)(2,1)}, u32[]{:S(2)}) copy-start(bf16[1,512,1024]{2,1,0:T(8,128)(2,1)} %param.14) | copy-start | bytes 3145732
  6.5 53.1 %copy-start.1 = (bf16[1,512,1024]{2,1,0:T(8,128)(2,1)S(1)}, bf16[1,512,1024]{2,1,0:T(8,128)(2,1)}, u32[]{:S(2)}) copy-start(bf16[1,512,1024]{2,1,0:T(8,128)(2,1)} %param.15) | copy-start | bytes 3145732
  39.9 20.0 %all-to-all-start.1 = ((bf16[16,1,128]{2,1,0:T(2,128)(2,1)}), bf16[16,1,128]{2,1,0:T(2,128)(2,1)S(1)}, u32[]{:S(2)}, u32[]{:S(2)}) async-start(bf16[16,1,128]{2,1,0:T(2,128)(2,1)} %copy.21), calls=%async_computation.1 | async-start | bytes 16384 | tf_op jit(solution)/shard_map/all_to_all | solution.py:94
  43.4 54.6 %copy-start.3 = (u32[32]{0:T(128)S(1)}, u32[32]{0:T(128)}, u32[]{:S(2)}) copy-start(u32[32]{0:T(128)} %constant.25) | copy-start | bytes 388
  43.4 145.1 %copy-start.2 = (bf16[1,16384]{1,0:T(2,128)(2,1)S(1)}, bf16[1,16384]{1,0:T(2,128)(2,1)}, u32[]{:S(2)}) copy-start(bf16[1,16384]{1,0:T(2,128)(2,1)} %param.9) | copy-start | bytes 98308
  59.9 12.6 %all-to-all-start = ((bf16[16,2,512]{2,1,0:T(2,128)(2,1)}), bf16[16,2,512]{2,1,0:T(2,128)(2,1)S(1)}, u32[]{:S(2)}, u32[]{:S(2)}) async-start(bf16[16,2,512]{2,1,0:T(2,128)(2,1)} %reshape.201), calls=%async_computation | async-start | bytes 65536 | tf_op jit(solution)/shard_map/all_to_all | solution.py:93
  65.9 122.6 %all-reduce.3.cloned.1.call-start = ((), (), s32[]{:S(2)}) async-start(), calls=%async_computation.3 | async-start | bytes 2097152
Sparse Core Ops, SparseCore 0:
  98.1 90.3 all-reduce.2
where the time goes:
time: 198 us
  waiting for transfers between devices  96.4 us (49%)
  blocking collectives  35.4 us (18%)
  matrix products  30.8 us (16%)
  between operations  15.6 us (8%)
  starting transfers between devices  9.51 us (5%)
  other arithmetic  7.04 us (4%)
  local copies, waits for them, and re-layouts  3 us (2%)
    unnamed x2, waiting for transfers between devices  89.9 us
    all_gather x1, blocking collectives, per_device(): piece = lax.all_gather(normed, 'wide', axis=0, tiled=True)  26.2 us
    dot_general x1, matrix products, per_device(): jnp.dot(by_heads, out_weight, preferred_element_type=jnp.float32)  13.9 us
    dot_general x1, matrix products, per_device(): jnp.dot(piece, query_weight, preferred_element_type=jnp.float32)  12.9 us
    all_to_all x1, blocking collectives, per_device(): lax.all_to_all(attended, 'wide', split_axis=1, concat_axis=0, tiled=True)  9.2 us
    all_to_all x1, waiting for transfers between devices, per_device(): lax.all_to_all(projected[:, :query_cols], 'wide', split_axis=0, concat_ax...  6.41 us
    all_to_all x1, starting transfers between devices, per_device(): lax.all_to_all(projected[:, :query_cols], 'wide', split_axis=0, concat_ax...  5.98 us
  transfers between devices with their start and end apart: 3, of which 2 were waited for; matrix products, arithmetic and copies ran while one was open for 8% of the time, Pallas kernels for 0%

commit v1 on v0

--- a/solution.py
+++ b/solution.py
@@ -3,11 +3,14 @@
 import jax
 import jax.numpy as jnp
 from jax import lax
+from jax.experimental import pallas as pl
+from jax.experimental.pallas import tpu as pltpu
 from jax.sharding import PartitionSpec as P
 
 HQ = 128
 KVH = 8
 HD = 128
+GROUP = 16
 
 
 def rms_scale(inputs_wide, norm_gain):
@@ -104,9 +107,509 @@
     return (inputs_wide + summed).astype(jnp.bfloat16)
 
 
+LINE, PAIR, CORES = 4, 2, 2
+WIDE = LINE * PAIR * CORES
+TILE = 1024
+SLOTS = 24
+LANES = 128
+STEPS = 8
+
+
+def remote(source, target, sent, landed, peer):
+    return pltpu.make_async_remote_copy(
+        src_ref=source,
+        dst_ref=target,
+        send_sem=sent,
+        recv_sem=landed,
+        device_id={"wide": peer},
+        device_id_type=pl.DeviceIdType.MESH,
+    )
+
+
+def turn(values, cosine, sine):
+    return values * cosine + pltpu.roll(values, HD // 2, 1) * sine
+
+
+def fused_kernel(
+    lengths,
+    positions,
+    hidden,
+    gain,
+    wq,
+    wkv,
+    wo,
+    keys,
+    values,
+    out,
+    ring,
+    kv_held,
+    keys_held,
+    values_held,
+    rows_f32,
+    gain_f32,
+    normed,
+    tokens,
+    total,
+    message,
+    message_out,
+    message_in,
+    heads_out,
+    heads_in,
+    mixed,
+    partial,
+    from_core,
+    keep,
+    pair_out,
+    pair_in,
+    line_out,
+    line_in,
+    ring_sem,
+    kv_sem,
+    cache_sem,
+    norm_line_sent,
+    norm_pair_sent,
+    norm_core_sent,
+    norm_landed,
+    query_sent,
+    query_landed,
+    heads_sent,
+    heads_landed,
+    core_sent,
+    core_landed,
+    pair_sent,
+    pair_landed,
+    line_sent,
+    line_landed,
+):
+    me = lax.axis_index("wide")
+    core = lax.rem(me, CORES)
+    row = lax.rem(me // CORES, PAIR)
+    line = me // (CORES * PAIR)
+
+    def at(a_line, a_row, a_core):
+        return (a_line * PAIR + a_row) * CORES + a_core
+
+    def by_core(place):
+        return (
+            lax.rem(place, CORES) * (PAIR * LINE)
+            + lax.rem(place // CORES, PAIR) * LINE
+            + place // (CORES * PAIR)
+        )
+
+    other_core = at(line, row, 1 - core)
+    other_row = at(line, 1 - row, core)
+
+    def other_line(step):
+        return at(lax.rem(line + step, LINE), row, core)
+
+    def query_block(index):
+        return pltpu.make_async_copy(
+            wq.at[pl.ds(index * TILE, TILE), :], ring.at[index], ring_sem.at[index]
+        )
+
+    def out_block(index):
+        slot = lax.rem(index + 16, SLOTS)
+        return pltpu.make_async_copy(
+            wo.at[:, pl.ds(pl.multiple_of(index * TILE, TILE), TILE)],
+            ring.at[slot],
+            ring_sem.at[slot],
+        )
+
+    barrier = pltpu.get_barrier_semaphore()
+    for step in range(1, WIDE):
+        pl.semaphore_signal(
+            barrier,
+            inc=1,
+            device_id={"wide": lax.rem(me + step, WIDE)},
+            device_id_type=pl.DeviceIdType.MESH,
+        )
+
+    kv_copy = pltpu.make_async_copy(wkv, kv_held, kv_sem)
+    kv_copy.start()
+    for index in range(16):
+        query_block(index).start()
+    keys_copy = pltpu.make_async_copy(keys.at[0], keys_held, cache_sem.at[0])
+    values_copy = pltpu.make_async_copy(values.at[0], values_held, cache_sem.at[1])
+    keys_copy.start()
+    values_copy.start()
+    for index in range(SLOTS - 16):
+        out_block(index).start()
+
+    for part in range(16):
+        span = slice(part * TILE, (part + 1) * TILE)
+        rows_f32[part : part + 1, :] = hidden[:, span].astype(jnp.float32)
+        gain_f32[part : part + 1, :] = gain[:, span]
+    token = rows_f32[...]
+    spread = jnp.sum(token * token, keepdims=True) * (1.0 / (16 * TILE))
+    normed[me] = (token * lax.rsqrt(spread + 1e-05) * gain_f32[...]).astype(jnp.bfloat16)
+    pl.semaphore_wait(barrier, WIDE - 1)
+
+    def gather_line(step):
+        return remote(
+            normed.at[me],
+            normed.at[me],
+            norm_line_sent.at[step - 1],
+            norm_landed.at[me],
+            other_line(step),
+        )
+
+    def gather_pair(step):
+        place = other_line(step)
+        return remote(
+            normed.at[place],
+            normed.at[place],
+            norm_pair_sent.at[step],
+            norm_landed.at[place],
+            other_row,
+        )
+
+    def gather_core(step, a_row):
+        place = at(lax.rem(line + step, LINE), a_row, core)
+        return remote(
+            normed.at[place],
+            normed.at[place],
+            norm_core_sent.at[step * PAIR + a_row],
+            norm_landed.at[place],
+            other_core,
+        )
+
+    def landed(place):
+        remote(
+            normed.at[place],
+            normed.at[place],
+            norm_pair_sent.at[0],
+            norm_landed.at[place],
+            other_row,
+        ).wait_recv()
+
+    def spread_rows(place):
+        block = normed[place].astype(jnp.float32)
+        for part in range(TILE // LANES):
+            tokens[part, pl.ds(place, 16, stride=16), :] = block[:, part * LANES : (part + 1) * LANES]
+
+    for step in (2, 1, 3):
+        gather_line(step).start()
+    gather_pair(0).start()
+    gather_core(0, row).start()
+    spread_rows(me)
+    for step in (1, 3, 2):
+        landed(other_line(step))
+        gather_pair(step).start()
+        gather_core(step, row).start()
+        spread_rows(other_line(step))
+    for step in (0, 1, 3, 2):
+        place = at(lax.rem(line + step, LINE), 1 - row, core)
+        landed(place)
+        gather_core(step, 1 - row).start()
+        spread_rows(place)
+    for step in range(LINE):
+        for a_row in range(PAIR):
+            place = at(lax.rem(line + step, LINE), a_row, 1 - core)
+            landed(place)
+            spread_rows(place)
+
+    total[...] = jnp.zeros_like(total)
+    message[...] = jnp.zeros_like(message)
+    kv_copy.wait()
+
+    def project(index, carry):
+        rows = pl.ds(pl.multiple_of(index * 16, 16), 16)
+        tile = jnp.concatenate([tokens[part, rows, :] for part in range(TILE // LANES)], axis=1)
+        tile = tile.astype(jnp.bfloat16)
+        total[:, TILE:] += jnp.dot(
+            tile,
+            kv_held[pl.ds(pl.multiple_of(index * TILE, TILE), TILE), :],
+            preferred_element_type=jnp.float32,
+        )
+        query_block(index).wait()
+        total[:, :TILE] += jnp.dot(tile, ring[index], preferred_element_type=jnp.float32)
+
+        @pl.when(index < 32 - SLOTS)
+        def _():
+            out_block(index + SLOTS - 16).start()
+
+        return carry
+
+    lax.fori_loop(0, 16, project, 0)
+    for part in range(9):
+        message[pl.ds(part, 16, stride=16), :] = total[:, part * LANES : (part + 1) * LANES]
+    message_out[...] = message[...].astype(jnp.bfloat16).reshape(WIDE, 16, LANES)
+
+    def query_copy(step):
+        peer = lax.rem(me + step, WIDE)
+        return remote(
+            message_out.at[peer],
+            message_in.at[me],
+            query_sent.at[step],
+            query_landed.at[me],
+            peer,
+        )
+
+    for step in range(1, WIDE):
+        query_copy(step).start()
+    message_in[me] = message_out[me]
+
+    index = lax.broadcasted_iota(jnp.int32, (1, HD), 1)
+    lower = index < HD // 2
+    exponent = jnp.where(lower, index, index - HD // 2).astype(jnp.float32)
+    inverse = jnp.exp(exponent * (-2.0 * math.log(500000.0) / HD))
+    angle = positions[0].astype(jnp.float32) * inverse
+    cosine = jnp.cos(angle)
+    sine = jnp.sin(angle)
+    sine = jnp.where(lower, -sine, sine)
+    visible = lax.broadcasted_iota(jnp.int32, (GROUP, keys_held.shape[0]), 1) < lengths[0]
+    factor = 1.0 / math.sqrt(HD)
+    keys_copy.wait()
+    values_copy.wait()
+    for step in range(1, WIDE):
+        place = lax.rem(me + step, WIDE)
+        remote(
+            message_out.at[place],
+            message_in.at[place],
+            query_sent.at[step],
+            query_landed.at[place],
+            place,
+        ).wait_recv()
+    for head in range(KVH):
+        span = slice(head * HD, (head + 1) * HD)
+        one = message_in[2 * head].astype(jnp.float32)
+        two = message_in[2 * head + 1].astype(jnp.float32)
+        query = turn(jnp.concatenate([one[:8], two[:8]], axis=0), cosine, sine).astype(jnp.bfloat16)
+        new_key = message_in[head].astype(jnp.float32)[8:]
+        new_key = turn(new_key, cosine, sine)[:1].astype(jnp.bfloat16).astype(jnp.float32)
+        new_value = message_in[KVH + head].astype(jnp.float32)[8:9]
+        scores = factor * lax.dot_general(
+            query,
+            keys_held[:, span],
+            (((1,), (1,)), ((), ())),
+            preferred_element_type=jnp.float32,
+        )
+        scores = jnp.where(visible, scores, -1e30)
+        fresh = factor * jnp.sum(query.astype(jnp.float32) * new_key, axis=1, keepdims=True)
+        highest = jnp.maximum(jnp.max(scores, axis=1, keepdims=True), fresh)
+        raised = jnp.exp(scores - highest)
+        fresh = jnp.exp(fresh - highest)
+        whole = jnp.sum(raised, axis=1, keepdims=True) + fresh
+        weights = (raised / whole).astype(jnp.bfloat16)
+        fresh = (fresh / whole).astype(jnp.bfloat16).astype(jnp.float32)
+        attended = jnp.dot(weights, values_held[:, span], preferred_element_type=jnp.float32)
+        attended = (attended + fresh * new_value).astype(jnp.bfloat16).astype(jnp.float32)
+        heads_out[2 * head] = attended[:8]
+        heads_out[2 * head + 1] = attended[8:]
+
+    def heads_copy(step):
+        peer = lax.rem(me + step, WIDE)
+        return remote(
+            heads_out.at[peer],
+            heads_in.at[pl.ds(pl.multiple_of(by_core(me) * 8, 8), 8), :],
+            heads_sent.at[step],
+            heads_landed.at[me],
+            peer,
+        )
+
+    for step in range(1, WIDE):
+        heads_copy(step).start()
+    heads_in[pl.ds(pl.multiple_of(by_core(me) * 8, 8), 8), :] = heads_out[me]
+    for step in range(1, WIDE):
+        place = lax.rem(me + step, WIDE)
+        remote(
+            heads_out.at[place],
+            heads_in.at[pl.ds(pl.multiple_of(by_core(place) * 8, 8), 8), :],
+            heads_sent.at[step],
+            heads_landed.at[place],
+            place,
+        ).wait_recv()
+    mixed[...] = jnp.concatenate(
+        [heads_in[pl.ds(part, 16, stride=8), :] for part in range(8)], axis=1
+    ).astype(jnp.bfloat16)
+
+    half = 8 * 16
+    quarter = 4 * 16
+
+    def core_copy(chunk):
+        away = pl.ds(pl.multiple_of((1 - core) * half, half), half)
+        return remote(
+            partial.at[chunk, away, :],
+            from_core.at[chunk],
+            core_sent.at[chunk],
+            core_landed.at[chunk],
+            other_core,
+        )
+
+    def pair_copy(chunk):
+        return remote(
+            pair_out.at[chunk],
+            pair_in.at[chunk],
+            pair_sent.at[chunk],
+            pair_landed.at[chunk],
+            other_row,
+        )
+
+    def line_copy(chunk, step):
+        goal = lax.rem(line + step, LINE)
+        return remote(
+            line_out.at[chunk, goal],
+            line_in.at[chunk, step - 1],
+            line_sent.at[chunk, step - 1],
+            line_landed.at[chunk, step - 1],
+            other_line(step),
+        )
+
+    def multiply(chunk):
+        for side in range(2):
+            number = chunk * 2 + side
+            out_block(number).wait()
+            slot = lax.rem(number + 16, SLOTS)
+            product = jnp.dot(mixed[...], ring[slot], preferred_element_type=jnp.float32)
+            for part in range(TILE // LANES):
+                partial[chunk, pl.ds(side * 8 + part, 16, stride=16), :] = product[
+                    :, part * LANES : (part + 1) * LANES
+                ]
+        core_copy(chunk).start()
+
+    def over_cores(chunk):
+        core_copy(chunk).wait_recv()
+        away, home = (1 - row) * quarter, row * quarter
+        base = core * half
+        pair_out[chunk] = (
+            partial[chunk, pl.ds(pl.multiple_of(base + away, quarter), quarter), :]
+            + from_core[chunk, pl.ds(pl.multiple_of(away, quarter), quarter), :]
+        ).astype(jnp.bfloat16)
+        pair_copy(chunk).start()
+        keep[chunk] = (
+            partial[chunk, pl.ds(pl.multiple_of(base + home, quarter), quarter), :]
+            + from_core[chunk, pl.ds(pl.multiple_of(home, quarter), quarter), :]
+        )
+
+    def over_pair(chunk):
+        pair_copy(chunk).wait_recv()
+        added = keep[chunk] + pair_in[chunk].astype(jnp.float32)
+        keep[chunk] = added
+        line_out[chunk] = added.astype(jnp.bfloat16).reshape(LINE, 16, LANES)
+        for step in (2, 1, 3):
+            line_copy(chunk, step).start()
+
+    def over_line(chunk):
+        for step in range(1, LINE):
+            line_copy(chunk, step).wait_recv()
+        added = keep[chunk, pl.ds(pl.multiple_of(line * 16, 16), 16), :]
+        for step in range(1, LINE):
+            added = added + line_in[chunk, step - 1].astype(jnp.float32)
+        out[pl.ds(pl.multiple_of(chunk * 16, 16), 16), :] = added
+
+    def stage(time, carry):
+        pl.when(time < STEPS)(lambda: multiply(time))
+        pl.when((time >= 1) & (time < STEPS + 1))(lambda: over_cores(time - 1))
+        pl.when((time >= 2) & (time < STEPS + 2))(lambda: over_pair(time - 2))
+        pl.when(time >= 3)(lambda: over_line(time - 3))
+        return carry
+
+    lax.fori_loop(0, STEPS + 3, stage, 0)
+
+    for step in range(1, LINE):
+        gather_line(step).wait_send()
+    for step in range(LINE):
+        gather_pair(step).wait_send()
+        for a_row in range(PAIR):
+            gather_core(step, a_row).wait_send()
+    for step in range(1, WIDE):
+        query_copy(step).wait_send()
+        heads_copy(step).wait_send()
+
+    def drain(chunk, carry):
+        core_copy(chunk).wait_send()
+        pair_copy(chunk).wait_send()
+        for step in range(1, LINE):
+            line_copy(chunk, step).wait_send()
+        return carry
+
+    lax.fori_loop(0, STEPS, drain, 0)
+
+
+def per_device_fused(
+    hidden_in,
+    norm_gain,
+    query_weight,
+    kv_weight,
+    out_weight,
+    cache_keys,
+    cache_values,
+    lengths,
+    positions,
+):
+    slots = cache_keys.shape[1]
+    f32, bf16 = jnp.float32, jnp.bfloat16
+    vmem, dma = pltpu.VMEM, pltpu.SemaphoreType.DMA
+    summed = pl.pallas_call(
+        fused_kernel,
+        out_shape=jax.ShapeDtypeStruct((LANES, LANES), f32),
+        in_specs=[pl.BlockSpec(memory_space=pltpu.SMEM)] * 2
+        + [pl.BlockSpec(memory_space=pltpu.VMEM)] * 2
+        + [pl.BlockSpec(memory_space=pl.ANY)] * 5,
+        out_specs=pl.BlockSpec(memory_space=pltpu.VMEM),
+        scratch_shapes=[
+            vmem((SLOTS, TILE, TILE), bf16),
+            vmem((16 * TILE, LANES), bf16),
+            vmem((slots, KVH * HD), bf16),
+            vmem((slots, KVH * HD), bf16),
+            vmem((16, TILE), f32),
+            vmem((16, TILE), f32),
+            vmem((WIDE, 16, TILE), bf16),
+            vmem((TILE // LANES, 256, LANES), f32),
+            vmem((16, TILE + LANES), f32),
+            vmem((WIDE * 16, LANES), f32),
+            vmem((WIDE, 16, LANES), bf16),
+            vmem((WIDE, 16, LANES), bf16),
+            vmem((WIDE, 8, LANES), f32),
+            vmem((WIDE * 8, LANES), f32),
+            vmem((16, TILE), bf16),
+            vmem((STEPS, 256, LANES), f32),
+            vmem((STEPS, 128, LANES), f32),
+            vmem((STEPS, 64, LANES), f32),
+            vmem((STEPS, 64, LANES), bf16),
+            vmem((STEPS, 64, LANES), bf16),
+            vmem((STEPS, LINE, 16, LANES), bf16),
+            vmem((STEPS, LINE - 1, 16, LANES), bf16),
+            dma((SLOTS,)),
+            dma,
+            dma((2,)),
+            dma((LINE - 1,)),
+            dma((LINE,)),
+            dma((LINE * PAIR,)),
+            dma((WIDE,)),
+            dma((WIDE,)),
+            dma((WIDE,)),
+            dma((WIDE,)),
+            dma((WIDE,)),
+            dma((STEPS,)),
+            dma((STEPS,)),
+            dma((STEPS,)),
+            dma((STEPS,)),
+            dma((STEPS, LINE - 1)),
+            dma((STEPS, LINE - 1)),
+        ],
+        compiler_params=pltpu.CompilerParams(
+            collective_id=0, has_side_effects=True, vmem_limit_bytes=62 * 1024 * 1024
+        ),
+        name="decode_attention",
+    )(
+        lengths,
+        positions,
+        hidden_in,
+        norm_gain.reshape(1, -1),
+        query_weight,
+        kv_weight,
+        out_weight,
+        cache_keys,
+        cache_values,
+    )
+    return (hidden_in.astype(f32) + summed.reshape(1, -1)).astype(bf16)
+
+
 def solution(mesh):
+    body = per_device_fused if mesh.shape["wide"] == WIDE else per_device
     return jax.shard_map(
-        per_device,
+        body,
         mesh=mesh,
         in_specs=(
             P(("groups", "wide"), None),

time: 198 us -> 68.8 us (0.35)
  waiting for transfers between devices: 96.4 us -> 0 us
  Pallas kernels: 0 us -> 65.7 us
  blocking collectives: 35.4 us -> 0 us
  matrix products: 30.8 us -> 0 us
  between operations: 15.6 us -> 1.32 us
  starting transfers between devices: 9.51 us -> 0 us
  other arithmetic: 7.04 us -> 1.56 us
  local copies, waits for them, and re-layouts: 3 us -> 0.01 us
    unnamed x2 -> x0, waiting for transfers between devices: 89.9 us -> none
    pallas_call x0 -> x1, Pallas kernels: none -> 65.7 us  [per_device_fused(): pl.pallas_call(fused_kernel, out_shape=jax.ShapeDtypeStruct((LANES, LANES...]
    dot_general x6 -> x0, matrix products: 30.8 us -> none  [the longest x1 13.9 us: per_device(): jnp.dot(by_heads, out_weight, preferred_element_type=jnp.float32)]
    all_gather x1 -> x0, blocking collectives: 26.2 us -> none  [per_device(): piece = lax.all_gather(normed, 'wide', axis=0, tiled=True)]
    all_to_all x2 -> x0, starting transfers between devices: 9.47 us -> none  [the longest x1 5.98 us: per_device(): lax.all_to_all(projected[:, :query_cols], 'wide', split_axis=0, concat_ax...]
    all_to_all x1 -> x0, blocking collectives: 9.2 us -> none  [per_device(): lax.all_to_all(attended, 'wide', split_axis=1, concat_axis=0, tiled=True)]
    all_to_all x2 -> x0, waiting for transfers between devices: 6.41 us -> none  [the longest x1 6.41 us: per_device(): lax.all_to_all(projected[:, :query_cols], 'wide', split_axis=0, concat_ax...]
  transfers between devices with their start and end apart: 3 -> 0, of which waited for: 2 -> 0; matrix products, arithmetic and copies ran while one was open for 8% -> 0% of each run, Pallas kernels for 0% -> 0%
where the time goes in v1:
time: 68.8 us; the launch traced here: 68.6 us
  Pallas kernels  65.7 us (95%)
  other arithmetic  1.56 us (2%)
  between operations  1.32 us (2%)
    pallas_call x1, Pallas kernels, per_device_fused(): pl.pallas_call(fused_kernel, out_shape=jax.ShapeDtypeStruct((LANES, LANES...  65.7 us
    convert_element_type x1, other arithmetic, per_device_fused(): return (hidden_in.astype(f32) + summed.reshape(1, -1)).astype(bf16)  1.56 us

profile of v1, /device:TPU:0, one launch (start us, length us, event | category | flops | bytes accessed | tf_op | source)
XLA Modules:
  0.0 68.6 jit_solution(12557618128449230081)
XLA Ops:
  1.3 0.0 copy-start
  1.3 65.7 %decode_attention.1 = f32[128,128]{1,0:T(8,128)} custom-call(s32[1]{0:T(128)S(6)} %copy.10.lengths, s32[1]{0:T(128)S(6)} %copy.11.positions, bf16[1,16384]{1,0:T(2,128)(2,1)} %hidden.1, f32[1,16384]{1,0:T(1,128)} %bitcast.3, bf16[16384,1024]{1,0:T(8,128)(2,1)} %wq.1, bf16[16384,128]{1,0:T(8,128)(2,1)} %wkv.1, bf16[1024,16384]{1,0:T(8,128)(2,1)} %wo.1, ...), custom_call_target="tpu_custom_call" | custom-call | tf_op jit(solution)/shard_map/decode_attention/pallas_call | solution.py:543
  67.1 0.0 copy-done
  67.1 1.6 %add_convert_fusion = bf16[1,16384]{1,0:T(2,128)(2,1)} fusion(f32[1,16384]{1,0:T(1,128)} %bitcast.2, bf16[1,16384]{1,0:T(2,128)(2,1)S(1)} %copy-done), kind=kLoop, calls=%fused_computation | loop fusion | flops 49152 | bytes 131072 | tf_op jit(solution)/shard_map/convert_element_type | solution.py:606
Async XLA Ops:
  1.3 65.8 %copy-start = (bf16[1,16384]{1,0:T(2,128)(2,1)S(1)}, bf16[1,16384]{1,0:T(2,128)(2,1)}, u32[]{:S(2)}) copy-start(bf16[1,16384]{1,0:T(2,128)(2,1)} %hidden.1) | copy-start | bytes 98308

commit v2 on v1

--- a/solution.py
+++ b/solution.py
@@ -113,6 +113,7 @@
 SLOTS = 24
 LANES = 128
 STEPS = 8
+LAGS = (2, 5, 8)
 
 
 def remote(source, target, sent, landed, peer):
@@ -153,6 +154,7 @@
     message,
     message_out,
     message_in,
+    scores,
     heads_out,
     heads_in,
     mixed,
@@ -357,7 +359,7 @@
     cosine = jnp.cos(angle)
     sine = jnp.sin(angle)
     sine = jnp.where(lower, -sine, sine)
-    visible = lax.broadcasted_iota(jnp.int32, (GROUP, keys_held.shape[0]), 1) < lengths[0]
+    visible = lax.broadcasted_iota(jnp.int32, scores.shape, 1) < lengths[0]
     factor = 1.0 / math.sqrt(HD)
     keys_copy.wait()
     values_copy.wait()
@@ -370,37 +372,54 @@
             query_landed.at[place],
             place,
         ).wait_recv()
+    arrived = [message_in[place].astype(jnp.float32) for place in range(WIDE)]
+    query = turn(jnp.concatenate([block[:8] for block in arrived], axis=0), cosine, sine)
+    query = query.astype(jnp.bfloat16)
+    new_keys = jnp.concatenate([block[8:9] for block in arrived[:KVH]], axis=0)
+    new_keys = turn(new_keys, cosine, sine).astype(jnp.bfloat16).astype(jnp.float32)
+    new_values = jnp.concatenate([block[8:9] for block in arrived[KVH:]], axis=0)
+
+    def per_query(rows):
+        return jnp.concatenate(
+            [jnp.broadcast_to(rows[head : head + 1], (GROUP, HD)) for head in range(KVH)], axis=0
+        )
+
     for head in range(KVH):
-        span = slice(head * HD, (head + 1) * HD)
-        one = message_in[2 * head].astype(jnp.float32)
-        two = message_in[2 * head + 1].astype(jnp.float32)
-        query = turn(jnp.concatenate([one[:8], two[:8]], axis=0), cosine, sine).astype(jnp.bfloat16)
-        new_key = message_in[head].astype(jnp.float32)[8:]
-        new_key = turn(new_key, cosine, sine)[:1].astype(jnp.bfloat16).astype(jnp.float32)
-        new_value = message_in[KVH + head].astype(jnp.float32)[8:9]
-        scores = factor * lax.dot_general(
-            query,
-            keys_held[:, span],
+        rows = slice(head * GROUP, (head + 1) * GROUP)
+        scores[rows, :] = lax.dot_general(
+            query[rows],
+            keys_held[:, head * HD : (head + 1) * HD],
             (((1,), (1,)), ((), ())),
             preferred_element_type=jnp.float32,
         )
-        scores = jnp.where(visible, scores, -1e30)
-        fresh = factor * jnp.sum(query.astype(jnp.float32) * new_key, axis=1, keepdims=True)
-        highest = jnp.maximum(jnp.max(scores, axis=1, keepdims=True), fresh)
-        raised = jnp.exp(scores - highest)
-        fresh = jnp.exp(fresh - highest)
-        whole = jnp.sum(raised, axis=1, keepdims=True) + fresh
-        weights = (raised / whole).astype(jnp.bfloat16)
-        fresh = (fresh / whole).astype(jnp.bfloat16).astype(jnp.float32)
-        attended = jnp.dot(weights, values_held[:, span], preferred_element_type=jnp.float32)
-        attended = (attended + fresh * new_value).astype(jnp.bfloat16).astype(jnp.float32)
-        heads_out[2 * head] = attended[:8]
-        heads_out[2 * head + 1] = attended[8:]
+    fresh = factor * jnp.sum(
+        query.astype(jnp.float32) * per_query(new_keys), axis=1, keepdims=True
+    )
+    scored = jnp.where(visible, factor * scores[...], -1e30)
+    highest = jnp.maximum(jnp.max(scored, axis=1, keepdims=True), fresh)
+    raised = jnp.exp(scored - highest)
+    fresh = jnp.exp(fresh - highest)
+    whole = 1.0 / (jnp.sum(raised, axis=1, keepdims=True) + fresh)
+    weights = (raised * whole).astype(jnp.bfloat16)
+    fresh = (fresh * whole).astype(jnp.bfloat16).astype(jnp.float32)
+    attended = jnp.concatenate(
+        [
+            jnp.dot(
+                weights[head * GROUP : (head + 1) * GROUP],
+                values_held[:, head * HD : (head + 1) * HD],
+                preferred_element_type=jnp.float32,
+            )
+            for head in range(KVH)
+        ],
+        axis=0,
+    )
+    attended = attended + fresh * per_query(new_values)
+    heads_out[...] = attended.astype(jnp.bfloat16).astype(jnp.float32)
 
     def heads_copy(step):
         peer = lax.rem(me + step, WIDE)
         return remote(
-            heads_out.at[peer],
+            heads_out.at[pl.ds(pl.multiple_of(peer * 8, 8), 8), :],
             heads_in.at[pl.ds(pl.multiple_of(by_core(me) * 8, 8), 8), :],
             heads_sent.at[step],
             heads_landed.at[me],
@@ -409,11 +428,13 @@
 
     for step in range(1, WIDE):
         heads_copy(step).start()
-    heads_in[pl.ds(pl.multiple_of(by_core(me) * 8, 8), 8), :] = heads_out[me]
+    heads_in[pl.ds(pl.multiple_of(by_core(me) * 8, 8), 8), :] = heads_out[
+        pl.ds(pl.multiple_of(me * 8, 8), 8), :
+    ]
     for step in range(1, WIDE):
         place = lax.rem(me + step, WIDE)
         remote(
-            heads_out.at[place],
+            heads_out.at[pl.ds(pl.multiple_of(place * 8, 8), 8), :],
             heads_in.at[pl.ds(pl.multiple_of(by_core(place) * 8, 8), 8), :],
             heads_sent.at[step],
             heads_landed.at[place],
@@ -499,12 +520,11 @@
 
     def stage(time, carry):
         pl.when(time < STEPS)(lambda: multiply(time))
-        pl.when((time >= 1) & (time < STEPS + 1))(lambda: over_cores(time - 1))
-        pl.when((time >= 2) & (time < STEPS + 2))(lambda: over_pair(time - 2))
-        pl.when(time >= 3)(lambda: over_line(time - 3))
+        for lag, task in ((LAGS[0], over_cores), (LAGS[1], over_pair), (LAGS[2], over_line)):
+            pl.when((time >= lag) & (time < STEPS + lag))(lambda lag=lag, task=task: task(time - lag))
         return carry
 
-    lax.fori_loop(0, STEPS + 3, stage, 0)
+    lax.fori_loop(0, STEPS + LAGS[2], stage, 0)
 
     for step in range(1, LINE):
         gather_line(step).wait_send()
@@ -560,7 +580,8 @@
             vmem((WIDE * 16, LANES), f32),
             vmem((WIDE, 16, LANES), bf16),
             vmem((WIDE, 16, LANES), bf16),
-            vmem((WIDE, 8, LANES), f32),
+            vmem((HQ, slots), f32),
+            vmem((WIDE * 8, LANES), f32),
             vmem((WIDE * 8, LANES), f32),
             vmem((16, TILE), bf16),
             vmem((STEPS, 256, LANES), f32),

time: 68.8 us -> 58.4 us (0.85)
  Pallas kernels: 65.7 us -> 55.3 us
    pallas_call x1, Pallas kernels: 65.7 us -> 55.3 us  [per_device_fused(): pl.pallas_call(fused_kernel, out_shape=jax.ShapeDtypeStruct((LANES, LANES...]
where the time goes in v2:
time: 58.4 us; the launch traced here: 58.2 us
  Pallas kernels  55.3 us (95%)
  other arithmetic  1.56 us (3%)
  between operations  1.32 us (2%)
    pallas_call x1, Pallas kernels, per_device_fused(): pl.pallas_call(fused_kernel, out_shape=jax.ShapeDtypeStruct((LANES, LANES...  55.3 us
    convert_element_type x1, other arithmetic, per_device_fused(): return (hidden_in.astype(f32) + summed.reshape(1, -1)).astype(bf16)  1.56 us

profile of v2, /device:TPU:0, one launch (start us, length us, event | category | flops | bytes accessed | tf_op | source)
XLA Modules:
  0.0 58.2 jit_solution(8333066474556357507)
XLA Ops:
  1.3 0.0 copy-start
  1.3 55.3 %decode_attention.1 = f32[128,128]{1,0:T(8,128)} custom-call(s32[1]{0:T(128)S(6)} %copy.10.lengths, s32[1]{0:T(128)S(6)} %copy.11.positions, bf16[1,16384]{1,0:T(2,128)(2,1)} %hidden.1, f32[1,16384]{1,0:T(1,128)} %bitcast.3, bf16[16384,1024]{1,0:T(8,128)(2,1)} %wq.1, bf16[16384,128]{1,0:T(8,128)(2,1)} %wkv.1, bf16[1024,16384]{1,0:T(8,128)(2,1)} %wo.1, ...), custom_call_target="tpu_custom_call" | custom-call | tf_op jit(solution)/shard_map/decode_attention/pallas_call | solution.py:563
  56.6 0.0 copy-done
  56.6 1.6 %add_convert_fusion = bf16[1,16384]{1,0:T(2,128)(2,1)} fusion(f32[1,16384]{1,0:T(1,128)} %bitcast.2, bf16[1,16384]{1,0:T(2,128)(2,1)S(1)} %copy-done), kind=kLoop, calls=%fused_computation | loop fusion | flops 49152 | bytes 131072 | tf_op jit(solution)/shard_map/convert_element_type | solution.py:627
Async XLA Ops:
  1.3 55.3 %copy-start = (bf16[1,16384]{1,0:T(2,128)(2,1)S(1)}, bf16[1,16384]{1,0:T(2,128)(2,1)}, u32[]{:S(2)}) copy-start(bf16[1,16384]{1,0:T(2,128)(2,1)} %hidden.1) | copy-start | bytes 98308

commit v3 on v2

--- a/solution.py
+++ b/solution.py
@@ -108,12 +108,13 @@
 
 
 LINE, PAIR, CORES = 4, 2, 2
-WIDE = LINE * PAIR * CORES
+CHIPS = LINE * PAIR
+WIDE = CHIPS * CORES
 TILE = 1024
 SLOTS = 24
 LANES = 128
 STEPS = 8
-LAGS = (2, 5, 8)
+LAGS = (2, 6)
 
 
 def remote(source, target, sent, landed, peer):
@@ -160,11 +161,8 @@
     mixed,
     partial,
     from_core,
-    keep,
-    pair_out,
-    pair_in,
-    line_out,
-    line_in,
+    chip_out,
+    chip_in,
     ring_sem,
     kv_sem,
     cache_sem,
@@ -178,10 +176,8 @@
     heads_landed,
     core_sent,
     core_landed,
-    pair_sent,
-    pair_landed,
-    line_sent,
-    line_landed,
+    chip_sent,
+    chip_landed,
 ):
     me = lax.axis_index("wide")
     core = lax.rem(me, CORES)
@@ -200,6 +196,12 @@
 
     other_core = at(line, row, 1 - core)
     other_row = at(line, 1 - row, core)
+
+    chip = row * LINE + line
+
+    def on_chip(step, a_core):
+        place = lax.rem(chip + step, CHIPS)
+        return at(lax.rem(place, LINE), place // LINE, a_core)
 
     def other_line(step):
         return at(lax.rem(line + step, LINE), row, core)
@@ -234,8 +236,6 @@
     values_copy = pltpu.make_async_copy(values.at[0], values_held, cache_sem.at[1])
     keys_copy.start()
     values_copy.start()
-    for index in range(SLOTS - 16):
-        out_block(index).start()
 
     for part in range(16):
         span = slice(part * TILE, (part + 1) * TILE)
@@ -326,10 +326,7 @@
         query_block(index).wait()
         total[:, :TILE] += jnp.dot(tile, ring[index], preferred_element_type=jnp.float32)
 
-        @pl.when(index < 32 - SLOTS)
-        def _():
-            out_block(index + SLOTS - 16).start()
-
+        out_block(index).start()
         return carry
 
     lax.fori_loop(0, 16, project, 0)
@@ -444,8 +441,7 @@
         [heads_in[pl.ds(part, 16, stride=8), :] for part in range(8)], axis=1
     ).astype(jnp.bfloat16)
 
-    half = 8 * 16
-    quarter = 4 * 16
+    half = CHIPS * 16
 
     def core_copy(chunk):
         away = pl.ds(pl.multiple_of((1 - core) * half, half), half)
@@ -457,23 +453,13 @@
             other_core,
         )
 
-    def pair_copy(chunk):
+    def chip_copy(chunk, step):
         return remote(
-            pair_out.at[chunk],
-            pair_in.at[chunk],
-            pair_sent.at[chunk],
-            pair_landed.at[chunk],
-            other_row,
-        )
-
-    def line_copy(chunk, step):
-        goal = lax.rem(line + step, LINE)
-        return remote(
-            line_out.at[chunk, goal],
-            line_in.at[chunk, step - 1],
-            line_sent.at[chunk, step - 1],
-            line_landed.at[chunk, step - 1],
-            other_line(step),
+            chip_out.at[chunk, lax.rem(chip + step, CHIPS)],
+            chip_in.at[chunk, step - 1],
+            chip_sent.at[chunk, step - 1],
+            chip_landed.at[chunk, step - 1],
+            on_chip(step, core),
         )
 
     def multiply(chunk):
@@ -490,41 +476,31 @@
 
     def over_cores(chunk):
         core_copy(chunk).wait_recv()
-        away, home = (1 - row) * quarter, row * quarter
-        base = core * half
-        pair_out[chunk] = (
-            partial[chunk, pl.ds(pl.multiple_of(base + away, quarter), quarter), :]
-            + from_core[chunk, pl.ds(pl.multiple_of(away, quarter), quarter), :]
-        ).astype(jnp.bfloat16)
-        pair_copy(chunk).start()
-        keep[chunk] = (
-            partial[chunk, pl.ds(pl.multiple_of(base + home, quarter), quarter), :]
-            + from_core[chunk, pl.ds(pl.multiple_of(home, quarter), quarter), :]
-        )
-
-    def over_pair(chunk):
-        pair_copy(chunk).wait_recv()
-        added = keep[chunk] + pair_in[chunk].astype(jnp.float32)
-        keep[chunk] = added
-        line_out[chunk] = added.astype(jnp.bfloat16).reshape(LINE, 16, LANES)
-        for step in (2, 1, 3):
-            line_copy(chunk, step).start()
-
-    def over_line(chunk):
-        for step in range(1, LINE):
-            line_copy(chunk, step).wait_recv()
-        added = keep[chunk, pl.ds(pl.multiple_of(line * 16, 16), 16), :]
-        for step in range(1, LINE):
-            added = added + line_in[chunk, step - 1].astype(jnp.float32)
+        home = pl.multiple_of(core * half, half)
+        added = partial[chunk, pl.ds(home, half), :] + from_core[chunk]
+        chip_out[chunk] = added.astype(jnp.bfloat16).reshape(CHIPS, 16, LANES)
+        for step in range(1, CHIPS):
+            chip_copy(chunk, step).start()
+
+    def over_chips(chunk):
+        for step in range(1, CHIPS):
+            chip_copy(chunk, step).wait_recv()
+        own = pl.multiple_of(chip * 16, 16)
+        added = (
+            partial[chunk, pl.ds(pl.multiple_of(core * half + own, 16), 16), :]
+            + from_core[chunk, pl.ds(own, 16), :]
+        )
+        for step in range(1, CHIPS):
+            added = added + chip_in[chunk, step - 1].astype(jnp.float32)
         out[pl.ds(pl.multiple_of(chunk * 16, 16), 16), :] = added
 
     def stage(time, carry):
         pl.when(time < STEPS)(lambda: multiply(time))
-        for lag, task in ((LAGS[0], over_cores), (LAGS[1], over_pair), (LAGS[2], over_line)):
+        for lag, task in ((LAGS[0], over_cores), (LAGS[1], over_chips)):
             pl.when((time >= lag) & (time < STEPS + lag))(lambda lag=lag, task=task: task(time - lag))
         return carry
 
-    lax.fori_loop(0, STEPS + LAGS[2], stage, 0)
+    lax.fori_loop(0, STEPS + LAGS[1], stage, 0)
 
     for step in range(1, LINE):
         gather_line(step).wait_send()
@@ -538,9 +514,8 @@
 
     def drain(chunk, carry):
         core_copy(chunk).wait_send()
-        pair_copy(chunk).wait_send()
-        for step in range(1, LINE):
-            line_copy(chunk, step).wait_send()
+        for step in range(1, CHIPS):
+            chip_copy(chunk, step).wait_send()
         return carry
 
     lax.fori_loop(0, STEPS, drain, 0)
@@ -586,11 +561,8 @@
             vmem((16, TILE), bf16),
             vmem((STEPS, 256, LANES), f32),
             vmem((STEPS, 128, LANES), f32),
-            vmem((STEPS, 64, LANES), f32),
-            vmem((STEPS, 64, LANES), bf16),
-            vmem((STEPS, 64, LANES), bf16),
-            vmem((STEPS, LINE, 16, LANES), bf16),
-            vmem((STEPS, LINE - 1, 16, LANES), bf16),
+            vmem((STEPS, CHIPS, 16, LANES), bf16),
+            vmem((STEPS, CHIPS - 1, 16, LANES), bf16),
             dma((SLOTS,)),
             dma,
             dma((2,)),
@@ -604,10 +576,8 @@
             dma((WIDE,)),
             dma((STEPS,)),
             dma((STEPS,)),
-            dma((STEPS,)),
-            dma((STEPS,)),
-            dma((STEPS, LINE - 1)),
-            dma((STEPS, LINE - 1)),
+            dma((STEPS, CHIPS - 1)),
+            dma((STEPS, CHIPS - 1)),
         ],
         compiler_params=pltpu.CompilerParams(
             collective_id=0, has_side_effects=True, vmem_limit_bytes=62 * 1024 * 1024

time: 58.4 us -> 52.1 us (0.89)
  Pallas kernels: 55.3 us -> 49 us
    pallas_call x1, Pallas kernels: 55.3 us -> 49 us  [per_device_fused(): pl.pallas_call(fused_kernel, out_shape=jax.ShapeDtypeStruct((LANES, LANES...]
where the time goes in v3:
time: 52.1 us; the launch traced here: 51.9 us
  Pallas kernels  49 us (94%)
  other arithmetic  1.56 us (3%)
  between operations  1.32 us (3%)
    pallas_call x1, Pallas kernels, per_device_fused(): pl.pallas_call(fused_kernel, out_shape=jax.ShapeDtypeStruct((LANES, LANES...  49 us
    convert_element_type x1, other arithmetic, per_device_fused(): return (hidden_in.astype(f32) + summed.reshape(1, -1)).astype(bf16)  1.56 us

profile of v3, /device:TPU:0, one launch (start us, length us, event | category | flops | bytes accessed | tf_op | source)
XLA Modules:
  0.0 51.9 jit_solution(6285296746250447718)
XLA Ops:
  1.3 0.0 copy-start
  1.3 49.0 %decode_attention.1 = f32[128,128]{1,0:T(8,128)} custom-call(s32[1]{0:T(128)S(6)} %copy.10.lengths, s32[1]{0:T(128)S(6)} %copy.11.positions, bf16[1,16384]{1,0:T(2,128)(2,1)} %hidden.1, f32[1,16384]{1,0:T(1,128)} %bitcast.3, bf16[16384,1024]{1,0:T(8,128)(2,1)} %wq.1, bf16[16384,128]{1,0:T(8,128)(2,1)} %wkv.1, bf16[1024,16384]{1,0:T(8,128)(2,1)} %wo.1, ...), custom_call_target="tpu_custom_call" | custom-call | tf_op jit(solution)/shard_map/decode_attention/pallas_call | solution.py:538
  50.3 0.0 copy-done
  50.3 1.6 %add_convert_fusion = bf16[1,16384]{1,0:T(2,128)(2,1)} fusion(f32[1,16384]{1,0:T(1,128)} %bitcast.2, bf16[1,16384]{1,0:T(2,128)(2,1)S(1)} %copy-done), kind=kLoop, calls=%fused_computation | loop fusion | flops 49152 | bytes 131072 | tf_op jit(solution)/shard_map/convert_element_type | solution.py:597
Async XLA Ops:
  1.3 49.0 %copy-start = (bf16[1,16384]{1,0:T(2,128)(2,1)S(1)}, bf16[1,16384]{1,0:T(2,128)(2,1)}, u32[]{:S(2)}) copy-start(bf16[1,16384]{1,0:T(2,128)(2,1)} %hidden.1) | copy-start | bytes 98308
